TPU v7x, 256 devices: a whole 4x4x8 slice. The times are simulated.
256 devices in a mesh: wide: 128 (over z, y, x), narrow: 2 (over core).
Axes of the slice: x: 4, y: 4, z: 8, core: 2. Of those that a mesh axis runs over, the one named last changes fastest.
Arguments:
- vectors: bfloat16 [524288, 512], P(('wide', 'narrow')), may hold values from -6 to 6
- leaf_factors: bfloat16 [6, 8192, 64, 128], P(None, ('wide', 'narrow')), may hold values from -0.5 to 0.5
- root_factors: bfloat16 [6, 8192, 64, 128], P(None, ('wide', 'narrow')), may hold values from -0.5 to 0.5
Outputs:
- applied: bfloat16 [524288, 512], P(('wide', 'narrow'))
All inputs are finite; a program needn't handle non-finite values.
Results may differ from a plain program's by a relative error of at most 0.024.
Values may be sent and summed in bfloat16 or wider, within the bound.
A program may use at most 64 MiB of HBM per device.

v0:
```python
import jax
import jax.numpy as jnp
from jax import lax
from jax.sharding import PartitionSpec as P


def partner(block, axis, bit):
    count = lax.axis_size(axis)
    route = []
    for low in range(count):
        high = low | 1 << bit
        if high != low and high < count:
            route += [(low, high), (high, low)]
    return lax.ppermute(block, axis, route)


def partner_blocks(blocks, stride):
    block_count, block_rows, columns = blocks.shape
    grouped = blocks.reshape(block_count // (2 * stride), 2, stride, block_rows, columns)
    return grouped[:, ::-1].reshape(blocks.shape)


def apply_level(factor, blocks, paired):
    block_rows = blocks.shape[1]
    direct = jnp.einsum(
        "nij,njr->nir", factor[:, :, :block_rows], blocks, preferred_element_type=jnp.float32
    )
    crossed = jnp.einsum(
        "nij,njr->nir", factor[:, :, block_rows:], paired, preferred_element_type=jnp.float32
    )
    return (direct + crossed).astype(jnp.bfloat16)


def per_device(vectors, leaf_factors, root_factors):
    section_levels, block_count, block_rows, doubled = leaf_factors.shape
    local_levels = section_levels - 1
    blocks = vectors.reshape(block_count, block_rows, vectors.shape[1])
    for depth in range(local_levels):
        blocks = apply_level(leaf_factors[depth], blocks, partner_blocks(blocks, 2**depth))
    paired = partner(blocks, "narrow", 0)
    blocks = apply_level(leaf_factors[local_levels], blocks, paired)
    leafed = blocks.reshape(block_count * block_rows, vectors.shape[1])
    moved = lax.all_to_all(leafed, "wide", split_axis=0, concat_axis=0, tiled=True)
    section_blocks = moved.reshape(block_count, block_rows, moved.shape[1])
    partner_rows = partner(section_blocks, "narrow", 0)
    section_blocks = apply_level(root_factors[0], section_blocks, partner_rows)
    for depth in range(local_levels):
        section_blocks = apply_level(
            root_factors[depth + 1], section_blocks, partner_blocks(section_blocks, 2**depth)
        )
    return section_blocks.reshape(moved.shape)


def solution(mesh):
    in_specs = (
        P(("wide", "narrow"), None),
        P(None, ("wide", "narrow"), None, None),
        P(None, ("wide", "narrow"), None, None),
    )
    out_specs = P(("wide", "narrow"), None)
    return jax.shard_map(
        per_device, mesh=mesh, in_specs=in_specs, out_specs=out_specs, check_vma=False
    )
```

profile of v0, /device:TPU:1, one launch (start us, length us, event | category | flops | bytes accessed | tf_op | source)
XLA Modules:
  0.0 160.6 jit_solution(2826941734983580070)
XLA Ops:
  0.0 4.0 %slice_bitcast_fusion.6 = (bf16[32,64,128]{2,1,0:T(8,128)(2,1)S(1)}, bf16[32,64,128]{2,1,0:T(8,128)(2,1)}, bf16[32,64,128]{2,1,0:T(8,128)(2,1)}, bf16[32,64,128]...) fusion(bf16[6,32,64,128]{3,2,1,0:T(8,128)(2,1)} %param.4), kind=kLoop, calls=%fused_computation.54 | loop fusion | bytes 6291456 | tf_op jit(solution)/shard_map/squeeze | solution.py:41
  4.0 0.0 copy-done.1
  4.0 1.5 rev.30
  5.5 1.9 %fusion.12 = f32[32,64,512]{2,1,0:T(8,128)S(1)} fusion(bf16[32,64,512]{2,1,0:T(8,128)(2,1)S(1)} %bitcast.115, bf16[32,64,128]{2,1,0:T(8,128)(2,1)} %get-tuple-element.15), kind=kOutput, calls=%fused_computation.24 | convolution fusion | flops 134217728 | bytes 6815744 | tf_op jit(solution)/shard_map/nij,njr->nir/dot_general | solution.py:25
  7.4 0.0 copy-done
  7.4 0.0 copy-done.8
  7.4 0.8 add_convert_fusion.11
  8.2 0.3 copy-done.7
  8.4 2.6 %fusion.14 = f32[32,512,64]{1,2,0:T(8,128)} fusion(bf16[32,64,512]{2,1,0:T(8,128)(2,1)S(1)} %add_convert_fusion.11, bf16[32,64,128]{2,1,0:T(8,128)(2,1)S(1)} %copy-done.7), kind=kOutput, calls=%fused_computation.26 | convolution fusion | flops 134217728 | bytes 6815744 | tf_op jit(solution)/shard_map/nij,njr->nir/dot_general | solution.py:25
  11.1 1.5 rev.31
  12.6 3.8 %add_convert_fusion.10 = bf16[32,512,64]{1,2,0:T(8,128)(2,1)S(1)} fusion(f32[32,512,64]{1,2,0:T(8,128)} %fusion.14, bf16[32,64,512]{2,1,0:T(8,128)(2,1)} %bitcast.103, bf16[32,64,128]{2,1,0:T(8,128)(2,1)} %get-tuple-element.14), kind=kOutput, calls=%fused_computation.10 | convolution fusion | flops 136314880 | bytes 8912896 | tf_op jit(solution)/shard_map/nij,njr->nir/dot_general | solution.py:28
  16.4 0.0 copy-done.5
  16.4 2.6 %fusion.16 = f32[32,512,64]{1,2,0:T(8,128)} fusion(bf16[32,512,64]{1,2,0:T(8,128)(2,1)S(1)} %add_convert_fusion.10, bf16[32,64,128]{2,1,0:T(8,128)(2,1)S(1)} %copy-done.5), kind=kOutput, calls=%fused_computation.28 | convolution fusion | flops 134217728 | bytes 6815744 | tf_op jit(solution)/shard_map/nij,njr->nir/dot_general | solution.py:25
  19.0 1.5 rev.32
  20.5 3.8 %add_convert_fusion.9 = bf16[32,512,64]{1,2,0:T(8,128)(2,1)S(1)} fusion(f32[32,512,64]{1,2,0:T(8,128)} %fusion.16, bf16[32,64,512]{2,1,0:T(8,128)(2,1)} %bitcast.104, bf16[32,64,128]{2,1,0:T(8,128)(2,1)} %get-tuple-element.13), kind=kOutput, calls=%fused_computation.9 | convolution fusion | flops 136314880 | bytes 8912896 | tf_op jit(solution)/shard_map/nij,njr->nir/dot_general | solution.py:28
  24.3 2.6 %fusion.18 = f32[32,512,64]{1,2,0:T(8,128)} fusion(bf16[32,512,64]{1,2,0:T(8,128)(2,1)S(1)} %add_convert_fusion.9, bf16[32,64,128]{2,1,0:T(8,128)(2,1)S(1)} %copy-done.3), kind=kOutput, calls=%fused_computation.30 | convolution fusion | flops 134217728 | bytes 6815744 | tf_op jit(solution)/shard_map/nij,njr->nir/dot_general | solution.py:25
  26.9 1.5 rev.33
  28.4 3.7 %add_convert_fusion.8 = bf16[32,512,64]{1,2,0:T(8,128)(2,1)S(1)} fusion(f32[32,512,64]{1,2,0:T(8,128)} %fusion.18, bf16[32,64,512]{2,1,0:T(8,128)(2,1)} %bitcast.105, bf16[32,64,128]{2,1,0:T(8,128)(2,1)} %get-tuple-element.12), kind=kOutput, calls=%fused_computation.8 | convolution fusion | flops 136314880 | bytes 8912896 | tf_op jit(solution)/shard_map/nij,njr->nir/dot_general | solution.py:28
  32.2 2.6 %fusion.20 = f32[32,512,64]{1,2,0:T(8,128)} fusion(bf16[32,512,64]{1,2,0:T(8,128)(2,1)S(1)} %add_convert_fusion.8, bf16[32,64,128]{2,1,0:T(8,128)(2,1)S(1)} %get-tuple-element.16), kind=kOutput, calls=%fused_computation.32 | convolution fusion | flops 134217728 | bytes 6815744 | tf_op jit(solution)/shard_map/nij,njr->nir/dot_general | solution.py:25
  34.8 1.5 rev.34
  36.3 3.6 %add_convert_fusion.7 = bf16[32,512,64]{1,2,0:T(8,128)(2,1)S(1)} fusion(f32[32,512,64]{1,2,0:T(8,128)} %fusion.20, bf16[32,64,512]{2,1,0:T(8,128)(2,1)} %bitcast.106, bf16[32,64,128]{2,1,0:T(8,128)(2,1)S(1)} %get-tuple-element.16), kind=kOutput, calls=%fused_computation.7 | convolution fusion | flops 136314880 | bytes 8912896 | tf_op jit(solution)/shard_map/nij,njr->nir/dot_general | solution.py:28
  39.9 3.4 %collective-permute-start = (bf16[32,64,512]{2,1,0:T(8,128)(2,1)S(1)}, bf16[32,64,512]{2,1,0:T(8,128)(2,1)S(1)}, u32[]{:S(2)}, u32[]{:S(2)}) collective-permute-start(bf16[32,64,512]{2,1,0:T(8,128)(2,1)S(1)} %bitcast.102), channel_id=1, source_target_pairs={{0,1},{1,0},{2,3},{3,2},{4,5},{5,4},{6,7},{7,6},{8,9},{9,8},{10,11... | collective-permute-start | bytes 6291464 | tf_op jit(solution)/shard_map/ppermute | solution.py:14
  43.2 0.7 fusion.22
  43.9 3.1 %collective-permute-done = bf16[32,64,512]{2,1,0:T(8,128)(2,1)S(1)} collective-permute-done((bf16[32,64,512]{2,1,0:T(8,128)(2,1)S(1)}, bf16[32,64,512]{2,1,0:T(8,128)(2,1)S(1)}, u32[]{:S(2)}, u32[]{:S(2)}) %collective-permute-start) | collective-permute-done | bytes 2097184 | tf_op jit(solution)/shard_map/ppermute | solution.py:14
  47.0 0.8 add_convert_fusion.6
  47.8 0.0 copy-start.9
  47.8 63.8 %all_to_all.9 = bf16[128,16,512]{2,1,0:T(8,128)(2,1)S(1)} all-to-all(bf16[128,16,512]{2,1,0:T(8,128)(2,1)S(1)} %bitcast.107), channel_id=1, replica_groups=mesh['wide'=128,'narrow'=2] {'wide'}, dimensions={0} | all-to-all | bytes 4194304 | tf_op jit(solution)/shard_map/all_to_all | solution.py:43
  111.6 3.9 %collective-permute-start.1 = (bf16[32,64,512]{2,1,0:T(8,128)(2,1)S(1)}, bf16[32,64,512]{2,1,0:T(8,128)(2,1)S(1)}, u32[]{:S(2)}, u32[]{:S(2)}) collective-permute-start(bf16[32,64,512]{2,1,0:T(8,128)(2,1)S(1)} %bitcast.116), channel_id=1, source_target_pairs={{0,1},{1,0},{2,3},{3,2},{4,5},{5,4},{6,7},{7,6},{8,9},{9,8},{10,11... | collective-permute-start | bytes 6291464 | tf_op jit(solution)/shard_map/ppermute | solution.py:14
  115.5 0.0 copy-done.9
  115.5 1.7 %slice_bitcast_fusion = (bf16[32,64,128]{2,1,0:T(8,128)(2,1)S(1)}, bf16[32,64,128]{2,1,0:T(8,128)(2,1)}, bf16[32,64,128]{2,1,0:T(8,128)(2,1)}, bf16[32,64,128]{2...) fusion(bf16[6,32,64,128]{3,2,1,0:T(8,128)(2,1)S(1)} %copy-done.9), kind=kLoop, calls=%fused_computation.48 | loop fusion | bytes 6291456 | tf_op jit(solution)/shard_map/squeeze | solution.py:49
  117.2 0.7 fusion.24
  117.9 1.4 collective-permute-done.1
  119.3 0.8 add_convert_fusion.5
  120.1 2.6 %fusion.26 = f32[32,512,64]{1,2,0:T(8,128)} fusion(bf16[32,512,64]{1,2,0:T(8,128)(2,1)S(1)} %add_convert_fusion.5, bf16[32,64,128]{2,1,0:T(8,128)(2,1)S(1)} %get-tuple-element.8), kind=kOutput, calls=%fused_computation.38 | convolution fusion | flops 134217728 | bytes 6815744 | tf_op jit(solution)/shard_map/nij,njr->nir/dot_general | solution.py:25
  122.7 1.5 rev.35
  124.2 3.8 %add_convert_fusion.4 = bf16[32,512,64]{1,2,0:T(8,128)(2,1)S(1)} fusion(f32[32,512,64]{1,2,0:T(8,128)} %fusion.26, bf16[32,64,512]{2,1,0:T(8,128)(2,1)} %bitcast.108, bf16[32,64,128]{2,1,0:T(8,128)(2,1)} %copy-done.6), kind=kOutput, calls=%fused_computation.4 | convolution fusion | flops 136314880 | bytes 8912896 | tf_op jit(solution)/shard_map/nij,njr->nir/dot_general | solution.py:28
  128.0 2.6 %fusion.28 = f32[32,512,64]{1,2,0:T(8,128)} fusion(bf16[32,512,64]{1,2,0:T(8,128)(2,1)S(1)} %add_convert_fusion.4, bf16[32,64,128]{2,1,0:T(8,128)(2,1)S(1)} %copy-done.4), kind=kOutput, calls=%fused_computation.40 | convolution fusion | flops 134217728 | bytes 6815744 | tf_op jit(solution)/shard_map/nij,njr->nir/dot_general | solution.py:25
  130.7 1.5 rev.36
  132.1 3.8 %add_convert_fusion.3 = bf16[32,512,64]{1,2,0:T(8,128)(2,1)S(1)} fusion(f32[32,512,64]{1,2,0:T(8,128)} %fusion.28, bf16[32,64,512]{2,1,0:T(8,128)(2,1)} %bitcast.109, bf16[32,64,128]{2,1,0:T(8,128)(2,1)} %get-tuple-element.7), kind=kOutput, calls=%fused_computation.3 | convolution fusion | flops 136314880 | bytes 8912896 | tf_op jit(solution)/shard_map/nij,njr->nir/dot_general | solution.py:28
  136.0 2.6 %fusion.30 = f32[32,512,64]{1,2,0:T(8,128)} fusion(bf16[32,512,64]{1,2,0:T(8,128)(2,1)S(1)} %add_convert_fusion.3, bf16[32,64,128]{2,1,0:T(8,128)(2,1)S(1)} %copy-done.2), kind=kOutput, calls=%fused_computation.42 | convolution fusion | flops 134217728 | bytes 6815744 | tf_op jit(solution)/shard_map/nij,njr->nir/dot_general | solution.py:25
  138.6 1.5 rev.37
  140.1 3.7 %add_convert_fusion.2 = bf16[32,512,64]{1,2,0:T(8,128)(2,1)S(1)} fusion(f32[32,512,64]{1,2,0:T(8,128)} %fusion.30, bf16[32,64,512]{2,1,0:T(8,128)(2,1)} %bitcast.110, bf16[32,64,128]{2,1,0:T(8,128)(2,1)} %get-tuple-element.6), kind=kOutput, calls=%fused_computation.2 | convolution fusion | flops 136314880 | bytes 8912896 | tf_op jit(solution)/shard_map/nij,njr->nir/dot_general | solution.py:28
  143.8 2.6 %fusion.32 = f32[32,512,64]{1,2,0:T(8,128)} fusion(bf16[32,512,64]{1,2,0:T(8,128)(2,1)S(1)} %add_convert_fusion.2, bf16[32,64,128]{2,1,0:T(8,128)(2,1)S(1)} %get-tuple-element.10), kind=kOutput, calls=%fused_computation.44 | convolution fusion | flops 134217728 | bytes 6815744 | tf_op jit(solution)/shard_map/nij,njr->nir/dot_general | solution.py:25
  146.5 1.5 rev.38
  148.0 3.6 %add_convert_fusion.1 = bf16[32,512,64]{1,2,0:T(8,128)(2,1)S(1)} fusion(f32[32,512,64]{1,2,0:T(8,128)} %fusion.32, bf16[32,64,512]{2,1,0:T(8,128)(2,1)} %bitcast.111, bf16[32,64,128]{2,1,0:T(8,128)(2,1)S(1)} %get-tuple-element.10), kind=kOutput, calls=%fused_computation.1 | convolution fusion | flops 136314880 | bytes 8912896 | tf_op jit(solution)/shard_map/nij,njr->nir/dot_general | solution.py:28
  151.5 2.6 %fusion.34 = f32[32,512,64]{1,2,0:T(8,128)} fusion(bf16[32,512,64]{1,2,0:T(8,128)(2,1)S(1)} %add_convert_fusion.1, bf16[32,64,128]{2,1,0:T(8,128)(2,1)S(1)} %get-tuple-element.5), kind=kOutput, calls=%fused_computation.46 | convolution fusion | flops 134217728 | bytes 6815744 | tf_op jit(solution)/shard_map/nij,njr->nir/dot_general | solution.py:25
  154.2 1.5 rev.39
  155.7 4.9 %add_convert_fusion = bf16[32,512,64]{1,2,0:T(8,128)(2,1)} fusion(f32[32,512,64]{1,2,0:T(8,128)} %fusion.34, bf16[32,64,512]{2,1,0:T(8,128)(2,1)} %bitcast.112, bf16[32,64,128]{2,1,0:T(8,128)(2,1)S(1)} %get-tuple-element.5), kind=kOutput, calls=%fused_computation | convolution fusion | flops 136314880 | bytes 8912896 | tf_op jit(solution)/shard_map/nij,njr->nir/dot_general | solution.py:28
  (13 shorter events, 0.0 us)
Async XLA Ops:
  0.0 4.0 %copy-start.1 = (bf16[2048,512]{1,0:T(8,128)(2,1)S(1)}, bf16[2048,512]{1,0:T(8,128)(2,1)}, u32[]{:S(2)}) copy-start(bf16[2048,512]{1,0:T(8,128)(2,1)} %param.3) | copy-start | bytes 6291460
  5.5 1.9 %copy-start = (bf16[16,2,1,64,512]{4,3,1,0,2:T(8,128)(2,1)S(1)}, bf16[16,2,1,64,512]{4,3,1,0,2:T(8,128)(2,1)}, u32[]{:S(2)}) copy-start(bf16[16,2,1,64,512]{4,3,1,0,2:T(8,128)(2,1)} %rev.30) | copy-start | bytes 6291460
  5.5 1.9 %copy-start.8 = (bf16[32,64,128]{2,1,0:T(8,128)(2,1)S(1)}, bf16[32,64,128]{2,1,0:T(8,128)(2,1)}, u32[]{:S(2)}) copy-start(bf16[32,64,128]{2,1,0:T(8,128)(2,1)} %get-tuple-element.15) | copy-start | bytes 1572868
  7.4 1.0 copy-start.7
  12.6 3.8 %copy-start.5 = (bf16[32,64,128]{2,1,0:T(8,128)(2,1)S(1)}, bf16[32,64,128]{2,1,0:T(8,128)(2,1)}, u32[]{:S(2)}) copy-start(bf16[32,64,128]{2,1,0:T(8,128)(2,1)} %get-tuple-element.13) | copy-start | bytes 1572868
  20.5 3.8 %copy-start.3 = (bf16[32,64,128]{2,1,0:T(8,128)(2,1)S(1)}, bf16[32,64,128]{2,1,0:T(8,128)(2,1)}, u32[]{:S(2)}) copy-start(bf16[32,64,128]{2,1,0:T(8,128)(2,1)} %get-tuple-element.12) | copy-start | bytes 1572868
  39.9 7.1 %collective-permute-start = (bf16[32,64,512]{2,1,0:T(8,128)(2,1)S(1)}, bf16[32,64,512]{2,1,0:T(8,128)(2,1)S(1)}, u32[]{:S(2)}, u32[]{:S(2)}) collective-permute-start(bf16[32,64,512]{2,1,0:T(8,128)(2,1)S(1)} %bitcast.102), channel_id=1, source_target_pairs={{0,1},{1,0},{2,3},{3,2},{4,5},{5,4},{6,7},{7,6},{8,9},{9,8},{10,11... | collective-permute-start | bytes 6291464 | tf_op jit(solution)/shard_map/ppermute | solution.py:14
  47.8 67.8 %copy-start.9 = (bf16[6,32,64,128]{3,2,1,0:T(8,128)(2,1)S(1)}, bf16[6,32,64,128]{3,2,1,0:T(8,128)(2,1)}, u32[]{:S(2)}) copy-start(bf16[6,32,64,128]{3,2,1,0:T(8,128)(2,1)} %param.5) | copy-start | bytes 9437188
  111.6 7.7 %collective-permute-start.1 = (bf16[32,64,512]{2,1,0:T(8,128)(2,1)S(1)}, bf16[32,64,512]{2,1,0:T(8,128)(2,1)S(1)}, u32[]{:S(2)}, u32[]{:S(2)}) collective-permute-start(bf16[32,64,512]{2,1,0:T(8,128)(2,1)S(1)} %bitcast.116), channel_id=1, source_target_pairs={{0,1},{1,0},{2,3},{3,2},{4,5},{5,4},{6,7},{7,6},{8,9},{9,8},{10,11... | collective-permute-start | bytes 6291464 | tf_op jit(solution)/shard_map/ppermute | solution.py:14
  117.2 2.9 %copy-start.6 = (bf16[32,64,128]{2,1,0:T(8,128)(2,1)}, bf16[32,64,128]{2,1,0:T(8,128)(2,1)S(1)}, u32[]{:S(2)}) copy-start(bf16[32,64,128]{2,1,0:T(8,128)(2,1)S(1)} %get-tuple-element.8) | copy-start | bytes 1572868
  124.2 3.8 %copy-start.4 = (bf16[32,64,128]{2,1,0:T(8,128)(2,1)S(1)}, bf16[32,64,128]{2,1,0:T(8,128)(2,1)}, u32[]{:S(2)}) copy-start(bf16[32,64,128]{2,1,0:T(8,128)(2,1)} %get-tuple-element.7) | copy-start | bytes 1572868
  132.1 3.8 %copy-start.2 = (bf16[32,64,128]{2,1,0:T(8,128)(2,1)S(1)}, bf16[32,64,128]{2,1,0:T(8,128)(2,1)}, u32[]{:S(2)}) copy-start(bf16[32,64,128]{2,1,0:T(8,128)(2,1)} %get-tuple-element.6) | copy-start | bytes 1572868
where the time goes:
time: 161 us
  matrix products  64 us (40%)
  blocking collectives  63.8 us (40%)
  local copies, waits for them, and re-layouts  20.8 us (13%)
  starting transfers between devices  7.28 us (5%)
  waiting for transfers between devices  4.54 us (3%)
    all_to_all x1, blocking collectives, per_device(): lax.all_to_all(leafed, 'wide', split_axis=0, concat_axis=0, tiled=True)  63.8 us
    dot_general x12, matrix products, apply_level(): jnp.einsum('nij,njr->nir', factor[:, :, block_rows:], paired, preferred_e...  37 us
    dot_general x12, matrix products, apply_level(): jnp.einsum('nij,njr->nir', factor[:, :, :block_rows], blocks, preferred_e...  27 us
    rev x10, local copies, waits for them, and re-layouts, partner_blocks(): return grouped[:, ::-1].reshape(blocks.shape)  14.8 us
    ppermute x2, starting transfers between devices, partner(): return lax.ppermute(block, axis, route)  7.28 us
    ppermute x2, waiting for transfers between devices, partner(): return lax.ppermute(block, axis, route)  4.54 us
    squeeze x1, local copies, waits for them, and re-layouts, per_device(): blocks = apply_level(leaf_factors[local_levels], blocks, paired)  4.01 us
  transfers between devices with their start and end apart: 2, of which 2 were waited for; matrix products, arithmetic and copies ran while one was open for 2% of the time, Pallas kernels for 0%

commit v1 on v0

v1 whole, which is shorter than its diff:
```python
import jax
import jax.numpy as jnp
from jax import lax
from jax.experimental import pallas as pl
from jax.experimental.pallas import tpu as pltpu
from jax.sharding import PartitionSpec as P

MESH = pl.DeviceIdType.MESH
NZ, NY, NX = 8, 4, 4
PLANE = NY * NX
BLOCKS, BLK, ROWS, COLS, CHUNKS = 32, 64, 16, 128, 4
GROUP = BLOCKS // NZ
LEVELS = 6
PLANE_FIRST = (False, False, True, True)
Z_ORDER = (4, 5, 1, 2, 6, 3, 7)


def swap_halves(factor):
    return jnp.concatenate([factor[:, BLK:], factor[:, :BLK]], axis=1)


def product(factor, blocks):
    return jnp.dot(factor, blocks, preferred_element_type=jnp.float32).astype(jnp.bfloat16)


def pair_level(factors, source, target, low, stride):
    high = low + stride
    out = product(
        jnp.concatenate([factors[low], factors[high]], axis=0),
        jnp.concatenate([source[low], source[high]], axis=0),
    )
    target[low] = out[:BLK]
    target[high] = out[BLK:]


def first_of_pair(index, stride):
    return (index // stride) * (2 * stride) + index % stride


def kernel(
    vectors, leaf_hbm, root_hbm, out_hbm,
    leaf, root, ping, pong, other, leafed, half, moved, moved_other, ping2, pong2, result,
    sem_vec, sem_leaf, sem_root, sem_out, sem_own,
    pair_send, pair_recv, z_send, z_recv, plane_send, plane_recv, pair2_send, pair2_recv,
):
    wide = lax.axis_index("wide")
    core = lax.axis_index("narrow")
    z, y, x = wide // PLANE, (wide // NX) % NY, wide % NX
    plane = wide % PLANE
    partner = (wide, 1 - core)

    def at_z(offset):
        return (z + offset) % NZ

    def z_device(offset):
        return (at_z(offset) * PLANE + plane, core)

    def plane_at(offset):
        return ((y + offset // NX) % NY) * NX + (x + offset % NX) % NX

    def plane_device(offset):
        return (z * PLANE + plane_at(offset), core)

    loads = []
    def load_vec(c):
        return pltpu.make_async_copy(
            vectors.at[:, :, pl.ds(c * COLS, COLS)], ping.at[c], sem_vec.at[c])

    def load_leaf(l):
        return pltpu.make_async_copy(leaf_hbm.at[l], leaf.at[l], sem_leaf.at[l])

    def load_root(l):
        return pltpu.make_async_copy(root_hbm.at[l], root.at[l], sem_root.at[l])

    load_vec(0).start()
    for l in range(LEVELS):
        load_leaf(l).start()
    for c in range(1, CHUNKS):
        load_vec(c).start()
    for l in range(LEVELS):
        load_root(l).start()

    barrier = pltpu.get_barrier_semaphore()
    pl.semaphore_signal(barrier, inc=1, device_id=partner, device_id_type=MESH)
    for d in range(1, NZ):
        pl.semaphore_signal(barrier, inc=1, device_id=z_device(d), device_id_type=MESH)

    @pl.loop(1, PLANE)
    def _(j):
        pl.semaphore_signal(barrier, inc=1, device_id=plane_device(j), device_id_type=MESH)

    def prepare(factors, stride):
        for q in range(BLOCKS // 2):
            high = first_of_pair(q, stride) + stride
            factors[high] = swap_halves(factors[high])

    def pair_copy(c, i, k):
        return pltpu.make_async_remote_copy(
            pong.at[c, :, pl.ds(i * GROUP, GROUP)], other.at[c, :, pl.ds(i * GROUP, GROUP)],
            pair_send.at[c, k], pair_recv.at[c, k], device_id=partner, device_id_type=MESH)

    def z_copy(c, d):
        source, target = (half, moved) if PLANE_FIRST[c] else (leafed, half)
        return pltpu.make_async_remote_copy(
            source.at[c, at_z(d)], target.at[c, z], z_send.at[c, d - 1], z_recv.at[c, d - 1],
            device_id=z_device(d), device_id_type=MESH)

    def z_own(c):
        source, target = (half, moved) if PLANE_FIRST[c] else (leafed, half)
        return pltpu.make_async_copy(source.at[c, z], target.at[c, z], sem_own.at[c, 0])

    def plane_copy(c, j):
        source, target = (leafed, half) if PLANE_FIRST[c] else (half, moved)
        return pltpu.make_async_remote_copy(
            source.at[c, :, plane_at(j)], target.at[c, :, plane], plane_send.at[c], plane_recv.at[c],
            device_id=plane_device(j), device_id_type=MESH)

    def plane_all(c):
        source, target = (leafed, half) if PLANE_FIRST[c] else (half, moved)
        return pltpu.make_async_remote_copy(
            source.at[c, :, pl.ds(0, PLANE - 1)], target.at[c, :, pl.ds(0, PLANE - 1)],
            plane_send.at[c], plane_recv.at[c], device_id=partner, device_id_type=MESH)

    def plane_own(c):
        source, target = (leafed, half) if PLANE_FIRST[c] else (half, moved)
        return pltpu.make_async_copy(source.at[c, :, plane], target.at[c, :, plane], sem_own.at[c, 1])

    def plane_start(c):
        @pl.loop(1, PLANE)
        def _(j):
            plane_copy(c, j).start()
        plane_own(c).start()

    def plane_wait(c):
        plane_own(c).wait()
        plane_all(c).wait_recv()

    def z_start(c):
        for d in Z_ORDER:
            z_copy(c, d).start()
        z_own(c).start()

    def pair2_copy(c, zs, k):
        return pltpu.make_async_remote_copy(
            moved.at[c, zs], moved_other.at[c, zs], pair2_send.at[c, k], pair2_recv.at[c, k],
            device_id=partner, device_id_type=MESH)

    def out_copy(c):
        return pltpu.make_async_copy(result.at[c], out_hbm.at[:, :, pl.ds(c * COLS, COLS)], sem_out.at[c])

    def whole_level(factors, source, target, stride):
        for q in range(BLOCKS // 2):
            pair_level(factors, source, target, first_of_pair(q, stride), stride)

    def leaf_levels(c):
        load_vec(c).wait()
        source, target = ping.at[c], pong.at[c]
        flat = pong.at[c]
        for l in range(4):
            if c == 0:
                load_leaf(l).wait()
                prepare(leaf.at[l], 1 << l)
            a = ping.at[c] if l % 2 == 0 else pong.at[c].reshape(BLOCKS, BLK, COLS)
            b = pong.at[c].reshape(BLOCKS, BLK, COLS) if l % 2 == 0 else ping.at[c]
            whole_level(leaf.at[l], a, b, 1 << l)
        if c == 0:
            load_leaf(4).wait()
            prepare(leaf.at[4], 16)
            load_leaf(5).wait()
            pl.semaphore_wait(barrier, 1 + (NZ - 1) + (PLANE - 1))
        for k in range(4):
            i = (z + k) % 4
            for q in range(GROUP):
                pair_level(leaf.at[4], ping.at[c], pong.at[c].reshape(BLOCKS, BLK, COLS), i * GROUP + q, 16)
            pair_copy(c, i, k).start()

    def leaf_last(c):
        mine = pong.at[c].reshape(BLOCKS, BLK, COLS)
        theirs = other.at[c].reshape(BLOCKS, BLK, COLS)
        target = leafed.at[c].reshape(BLOCKS, BLK, COLS)
        for k in range(4):
            pair_copy(c, (z + k) % 4, k).wait_recv()
            for d in (k + 4, k):
                for q in range(GROUP):
                    b = at_z(d) * GROUP + q
                    target[b] = product(leaf[5, b], jnp.concatenate([mine[b], theirs[b]], axis=0))
                if d != 0 and not PLANE_FIRST[c]:
                    z_copy(c, d).start()
        if PLANE_FIRST[c]:
            plane_start(c)
        else:
            z_own(c).start()

    def root_group(c, zs):
        mine = moved.at[c].reshape(BLOCKS, BLK, COLS)
        theirs = moved_other.at[c].reshape(BLOCKS, BLK, COLS)
        for q in range(GROUP):
            b = zs * GROUP + q
            ping2[b] = product(root[0, b], jnp.concatenate([mine[b], theirs[b]], axis=0))
        for q in (0, 2):
            pair_level(root.at[1], ping2, pong2, zs * GROUP + q, 1)
        for q in (0, 1):
            pair_level(root.at[2], pong2, ping2, zs * GROUP + q, 2)

    def root_rest(c):
        whole_level(root.at[3], ping2, pong2, 4)
        whole_level(root.at[4], pong2, ping2, 8)
        whole_level(root.at[5], ping2, result.at[c], 16)
        out_copy(c).start()

    def root_plane_last(c):
        plane_wait(c)
        for k in range(NZ):
            pair2_copy(c, k, k).start()
        for k in range(NZ):
            pair2_copy(c, k, k).wait_recv()
            root_group(c, k)
        root_rest(c)

    def root_z_last(c):
        order = (0,) + Z_ORDER
        for n, d in enumerate(order):
            if d == 0:
                z_own(c).wait()
            else:
                z_copy(c, d).wait_recv()
            pair2_copy(c, (z - d) % NZ, d).start()
            if n:
                e = order[n - 1]
                pair2_copy(c, (z - e) % NZ, e).wait_recv()
                root_group(c, (z - e) % NZ)
        e = order[-1]
        pair2_copy(c, (z - e) % NZ, e).wait_recv()
        root_group(c, (z - e) % NZ)
        root_rest(c)

    def z_wait(c):
        z_own(c).wait()
        for d in Z_ORDER:
            z_copy(c, d).wait_recv()

    for c in range(CHUNKS):
        leaf_levels(c)
        leaf_last(c)
    for l in range(LEVELS):
        load_root(l).wait()
        if l:
            prepare(root.at[l], 1 << (l - 1))

    z_wait(0)
    plane_start(0)
    plane_wait(2)
    z_start(2)
    z_wait(1)
    plane_start(1)
    plane_wait(3)
    z_start(3)
    root_plane_last(0)
    root_plane_last(1)
    root_z_last(2)
    root_z_last(3)

    for c in range(CHUNKS):
        for k in range(4):
            pair_copy(c, (z + k) % 4, k).wait_send()
        for d in Z_ORDER:
            z_copy(c, d).wait_send()
        plane_all(c).wait_send()
        for k in range(NZ):
            pair2_copy(c, k, k).wait_send()
        out_copy(c).wait()


def per_device(vectors, leaf_factors, root_factors):
    vectors = vectors.reshape(BLOCKS, BLK, CHUNKS * COLS)
    dma = pltpu.SemaphoreType.DMA
    wide_shape = (CHUNKS, BLOCKS, BLK, COLS)
    spread = (CHUNKS, NZ, PLANE, ROWS, COLS)
    halves = (CHUNKS, 2, BLOCKS // 2, BLK, COLS)
    bf = jnp.bfloat16
    vmem = pltpu.VMEM
    out = pl.pallas_call(
        kernel,
        out_shape=jax.ShapeDtypeStruct(vectors.shape, bf),
        in_specs=[pl.BlockSpec(memory_space=pl.ANY)] * 3,
        out_specs=pl.BlockSpec(memory_space=pl.ANY),
        scratch_shapes=[
            vmem((LEVELS, BLOCKS, BLK, 2 * BLK), bf),
            vmem((LEVELS, BLOCKS, BLK, 2 * BLK), bf),
            vmem(wide_shape, bf), vmem(halves, bf), vmem(halves, bf),
            vmem(spread, bf), vmem(spread, bf), vmem(spread, bf), vmem(spread, bf),
            vmem(wide_shape[1:], bf), vmem(wide_shape[1:], bf), vmem(wide_shape, bf),
            dma((CHUNKS,)), dma((LEVELS,)), dma((LEVELS,)), dma((CHUNKS,)), dma((CHUNKS, 2)),
            dma((CHUNKS, 4)), dma((CHUNKS, 4)), dma((CHUNKS, NZ - 1)), dma((CHUNKS, NZ - 1)),
            dma((CHUNKS,)), dma((CHUNKS,)), dma((CHUNKS, NZ)), dma((CHUNKS, NZ)),
        ],
        compiler_params=pltpu.CompilerParams(
            collective_id=0, has_side_effects=True, vmem_limit_bytes=48 * 1024 * 1024),
        name="butterfly",
    )(vectors, leaf_factors, root_factors)
    return out.reshape(BLOCKS * BLK, CHUNKS * COLS)


def solution(mesh):
    in_specs = (
        P(("wide", "narrow"), None),
        P(None, ("wide", "narrow"), None, None),
        P(None, ("wide", "narrow"), None, None),
    )
    out_specs = P(("wide", "narrow"), None)
    return jax.shard_map(
        per_device, mesh=mesh, in_specs=in_specs, out_specs=out_specs, check_vma=False
    )
```

time: 161 us -> 74.6 us (0.46)
  Pallas kernels: 0 us -> 71.6 us
  matrix products: 64 us -> 0 us
  blocking collectives: 63.8 us -> 0 us
  local copies, waits for them, and re-layouts: 20.8 us -> 2.91 us
  starting transfers between devices: 7.28 us -> 0 us
  waiting for transfers between devices: 4.54 us -> 0 us
    pallas_call x0 -> x1, Pallas kernels: none -> 71.6 us  [per_device(): pl.pallas_call(kernel, out_shape=jax.ShapeDtypeStruct(vectors.shape, bf),...]
    dot_general x24 -> x0, matrix products: 64 us -> none  [the longest x12 37 us: apply_level(): jnp.einsum('nij,njr->nir', factor[:, :, block_rows:], paired, preferred_e...]
    all_to_all x1 -> x0, blocking collectives: 63.8 us -> none  [per_device(): lax.all_to_all(leafed, 'wide', split_axis=0, concat_axis=0, tiled=True)]
    rev x10 -> x0, local copies, waits for them, and re-layouts: 14.8 us -> none  [partner_blocks(): return grouped[:, ::-1].reshape(blocks.shape)]
    ppermute x2 -> x0, starting transfers between devices: 7.28 us -> none  [partner(): return lax.ppermute(block, axis, route)]
    squeeze x2 -> x0, local copies, waits for them, and re-layouts: 5.68 us -> none  [the longest x1 4.01 us: per_device(): blocks = apply_level(leaf_factors[local_levels], blocks, paired)]
    ppermute x2 -> x0, waiting for transfers between devices: 4.54 us -> none  [partner(): return lax.ppermute(block, axis, route)]
    unnamed x20 -> x3, local copies, waits for them, and re-layouts: 0.31 us -> 2.91 us
  transfers between devices with their start and end apart: 2 -> 0, of which waited for: 2 -> 0; matrix products, arithmetic and copies ran while one was open for 2% -> 0% of each run, Pallas kernels for 0% -> 0%
where the time goes in v1:
time: 74.6 us; the launch traced here: 74.5 us
  Pallas kernels  71.6 us (96%)
  local copies, waits for them, and re-layouts  2.91 us (4%)
    pallas_call x1, Pallas kernels, per_device(): pl.pallas_call(kernel, out_shape=jax.ShapeDtypeStruct(vectors.shape, bf),...  71.6 us
    unnamed x3, local copies, waits for them, and re-layouts  2.91 us

profile of v1, /device:TPU:1, one launch (start us, length us, event | category | flops | bytes accessed | tf_op | source)
XLA Modules:
  0.0 74.5 jit_solution(16336262012666633308)
XLA Ops:
  0.0 0.0 copy-start
  0.0 1.6 %copy-done = bf16[2048,512]{1,0:T(8,128)(2,1)S(1)} copy-done((bf16[2048,512]{1,0:T(8,128)(2,1)S(1)}, bf16[2048,512]{1,0:T(8,128)(2,1)}, u32[]{:S(2)}) %copy-start) | copy-done | bytes 2097176
  1.6 71.6 %butterfly.1 = bf16[32,64,512]{2,1,0:T(8,128)(2,1)S(1)} custom-call(bf16[32,64,512]{2,1,0:T(8,128)(2,1)S(1)} %bitcast.3, bf16[6,32,64,128]{3,2,1,0:T(8,128)(2,1)} %leaf_hbm.1, bf16[6,32,64,128]{3,2,1,0:T(8,128)(2,1)} %root_hbm.1), custom_call_target="tpu_custom_call" | custom-call | tf_op jit(solution)/shard_map/butterfly/pallas_call | solution.py:282
  73.2 1.3 %copy.5 = bf16[2048,512]{1,0:T(8,128)(2,1)} copy(bf16[2048,512]{1,0:T(8,128)(2,1)S(1)} %bitcast.2) | data formatting | bytes 4194304
Async XLA Ops:
  0.0 1.6 %copy-start = (bf16[2048,512]{1,0:T(8,128)(2,1)S(1)}, bf16[2048,512]{1,0:T(8,128)(2,1)}, u32[]{:S(2)}) copy-start(bf16[2048,512]{1,0:T(8,128)(2,1)} %param.3) | copy-start | bytes 6291460

commit v2 on v1

--- a/solution.py
+++ b/solution.py
@@ -11,8 +11,13 @@
 BLOCKS, BLK, ROWS, COLS, CHUNKS = 32, 64, 16, 128, 4
 GROUP = BLOCKS // NZ
 LEVELS = 6
-PLANE_FIRST = (False, False, True, True)
-Z_ORDER = (4, 5, 1, 2, 6, 3, 7)
+PLANE_FIRST = (False, True, True, True)
+Z_ORDER = (4, 5, 3, 1, 7, 2, 6)
+FAR, NEAR = (4, 5, 3), (1, 7, 2, 6)
+BATCHES = ((0,) + FAR, NEAR)
+EARLY = 2
+RUN = ("L0", "L1", "L2", "L3", "P", "R0", "R1", "R2", "R3")
+own_copy = pltpu.make_async_copy
 
 
 def swap_halves(factor):
@@ -38,9 +43,9 @@
 
 
 def kernel(
-    vectors, leaf_hbm, root_hbm, out_hbm,
-    leaf, root, ping, pong, other, leafed, half, moved, moved_other, ping2, pong2, result,
-    sem_vec, sem_leaf, sem_root, sem_out, sem_own,
+    vectors, leaf_hbm, root_hbm, out,
+    leaf, root, ping, pong, other, leafed, half, moved, moved_other, ping2, pong2,
+    sem_vec, sem_leaf, sem_root, sem_own,
     pair_send, pair_recv, z_send, z_recv, plane_send, plane_recv, pair2_send, pair2_recv,
 ):
     wide = lax.axis_index("wide")
@@ -61,7 +66,6 @@
     def plane_device(offset):
         return (z * PLANE + plane_at(offset), core)
 
-    loads = []
     def load_vec(c):
         return pltpu.make_async_copy(
             vectors.at[:, :, pl.ds(c * COLS, COLS)], ping.at[c], sem_vec.at[c])
@@ -73,12 +77,8 @@
         return pltpu.make_async_copy(root_hbm.at[l], root.at[l], sem_root.at[l])
 
     load_vec(0).start()
-    for l in range(LEVELS):
+    for l in range(EARLY):
         load_leaf(l).start()
-    for c in range(1, CHUNKS):
-        load_vec(c).start()
-    for l in range(LEVELS):
-        load_root(l).start()
 
     barrier = pltpu.get_barrier_semaphore()
     pl.semaphore_signal(barrier, inc=1, device_id=partner, device_id_type=MESH)
@@ -107,7 +107,7 @@
 
     def z_own(c):
         source, target = (half, moved) if PLANE_FIRST[c] else (leafed, half)
-        return pltpu.make_async_copy(source.at[c, z], target.at[c, z], sem_own.at[c, 0])
+        return own_copy(source.at[c, z], target.at[c, z], sem_own.at[c, 0])
 
     def plane_copy(c, j):
         source, target = (leafed, half) if PLANE_FIRST[c] else (half, moved)
@@ -123,7 +123,7 @@
 
     def plane_own(c):
         source, target = (leafed, half) if PLANE_FIRST[c] else (half, moved)
-        return pltpu.make_async_copy(source.at[c, :, plane], target.at[c, :, plane], sem_own.at[c, 1])
+        return own_copy(source.at[c, :, plane], target.at[c, :, plane], sem_own.at[c, 1])
 
     def plane_start(c):
         @pl.loop(1, PLANE)
@@ -135,18 +135,14 @@
         plane_own(c).wait()
         plane_all(c).wait_recv()
 
-    def z_start(c):
-        for d in Z_ORDER:
+    def z_start(c, offsets):
+        for d in offsets:
             z_copy(c, d).start()
-        z_own(c).start()
 
     def pair2_copy(c, zs, k):
         return pltpu.make_async_remote_copy(
             moved.at[c, zs], moved_other.at[c, zs], pair2_send.at[c, k], pair2_recv.at[c, k],
             device_id=partner, device_id_type=MESH)
-
-    def out_copy(c):
-        return pltpu.make_async_copy(result.at[c], out_hbm.at[:, :, pl.ds(c * COLS, COLS)], sem_out.at[c])
 
     def whole_level(factors, source, target, stride):
         for q in range(BLOCKS // 2):
@@ -154,11 +150,12 @@
 
     def leaf_levels(c):
         load_vec(c).wait()
-        source, target = ping.at[c], pong.at[c]
-        flat = pong.at[c]
         for l in range(4):
             if c == 0:
                 load_leaf(l).wait()
+                if l == 0:
+                    for m in range(EARLY, LEVELS):
+                        load_leaf(m).start()
                 prepare(leaf.at[l], 1 << l)
             a = ping.at[c] if l % 2 == 0 else pong.at[c].reshape(BLOCKS, BLK, COLS)
             b = pong.at[c].reshape(BLOCKS, BLK, COLS) if l % 2 == 0 else ping.at[c]
@@ -167,6 +164,8 @@
             load_leaf(4).wait()
             prepare(leaf.at[4], 16)
             load_leaf(5).wait()
+            for m in range(1, CHUNKS):
+                load_vec(m).start()
             pl.semaphore_wait(barrier, 1 + (NZ - 1) + (PLANE - 1))
         for k in range(4):
             i = (z + k) % 4
@@ -178,60 +177,58 @@
         mine = pong.at[c].reshape(BLOCKS, BLK, COLS)
         theirs = other.at[c].reshape(BLOCKS, BLK, COLS)
         target = leafed.at[c].reshape(BLOCKS, BLK, COLS)
-        for k in range(4):
+        for k, offsets in enumerate(((4,), (5, 1), (6, 2), (7, 3, 0))):
             pair_copy(c, (z + k) % 4, k).wait_recv()
-            for d in (k + 4, k):
+            for d in offsets:
                 for q in range(GROUP):
                     b = at_z(d) * GROUP + q
                     target[b] = product(leaf[5, b], jnp.concatenate([mine[b], theirs[b]], axis=0))
                 if d != 0 and not PLANE_FIRST[c]:
                     z_copy(c, d).start()
-        if PLANE_FIRST[c]:
-            plane_start(c)
-        else:
+        if not PLANE_FIRST[c]:
             z_own(c).start()
 
-    def root_group(c, zs):
+    def root_groups(c, groups):
         mine = moved.at[c].reshape(BLOCKS, BLK, COLS)
         theirs = moved_other.at[c].reshape(BLOCKS, BLK, COLS)
-        for q in range(GROUP):
-            b = zs * GROUP + q
-            ping2[b] = product(root[0, b], jnp.concatenate([mine[b], theirs[b]], axis=0))
-        for q in (0, 2):
-            pair_level(root.at[1], ping2, pong2, zs * GROUP + q, 1)
-        for q in (0, 1):
-            pair_level(root.at[2], pong2, ping2, zs * GROUP + q, 2)
+        for zs in groups:
+            for q in range(GROUP):
+                b = zs * GROUP + q
+                ping2[b] = product(root[0, b], jnp.concatenate([mine[b], theirs[b]], axis=0))
+        for zs in groups:
+            for q in (0, 2):
+                pair_level(root.at[1], ping2, pong2, zs * GROUP + q, 1)
+        for zs in groups:
+            for q in (0, 1):
+                pair_level(root.at[2], pong2, ping2, zs * GROUP + q, 2)
 
     def root_rest(c):
         whole_level(root.at[3], ping2, pong2, 4)
         whole_level(root.at[4], pong2, ping2, 8)
-        whole_level(root.at[5], ping2, result.at[c], 16)
-        out_copy(c).start()
-
-    def root_plane_last(c):
-        plane_wait(c)
+        whole_level(root.at[5], ping2, out.at[:, :, pl.ds(c * COLS, COLS)], 16)
+
+    def root_exchange(c):
         for k in range(NZ):
             pair2_copy(c, k, k).start()
-        for k in range(NZ):
-            pair2_copy(c, k, k).wait_recv()
-            root_group(c, k)
+
+    def root_plane_last(c):
+        for batch in (range(4), range(4, 8)):
+            for k in batch:
+                pair2_copy(c, k, k).wait_recv()
+            root_groups(c, batch)
         root_rest(c)
 
     def root_z_last(c):
-        order = (0,) + Z_ORDER
-        for n, d in enumerate(order):
-            if d == 0:
-                z_own(c).wait()
-            else:
-                z_copy(c, d).wait_recv()
-            pair2_copy(c, (z - d) % NZ, d).start()
-            if n:
-                e = order[n - 1]
-                pair2_copy(c, (z - e) % NZ, e).wait_recv()
-                root_group(c, (z - e) % NZ)
-        e = order[-1]
-        pair2_copy(c, (z - e) % NZ, e).wait_recv()
-        root_group(c, (z - e) % NZ)
+        for batch in BATCHES:
+            for d in batch:
+                if d == 0:
+                    z_own(c).wait()
+                else:
+                    z_copy(c, d).wait_recv()
+                pair2_copy(c, (z - d) % NZ, d).start()
+            for d in batch:
+                pair2_copy(c, (z - d) % NZ, d).wait_recv()
+            root_groups(c, [(z - d) % NZ for d in batch])
         root_rest(c)
 
     def z_wait(c):
@@ -239,26 +236,51 @@
         for d in Z_ORDER:
             z_copy(c, d).wait_recv()
 
-    for c in range(CHUNKS):
-        leaf_levels(c)
-        leaf_last(c)
+    def leaf_section(c):
+        if f"L{c}" in RUN:
+            leaf_levels(c)
+            leaf_last(c)
+        else:
+            load_vec(c).wait()
+            if c == 0:
+                for l in range(LEVELS):
+                    load_leaf(l).wait()
+
+    def root_section(c):
+        if f"R{c}" in RUN:
+            (root_z_last if PLANE_FIRST[c] else root_plane_last)(c)
+
+    leaf_section(0)
+    for l in range(LEVELS):
+        load_root(l).start()
+    leaf_section(1)
+    plane_start(1)
+    leaf_section(2)
+    leaf_section(3)
     for l in range(LEVELS):
         load_root(l).wait()
-        if l:
+        if l and "P" in RUN:
             prepare(root.at[l], 1 << (l - 1))
-
+    plane_wait(1)
+    z_start(1, Z_ORDER)
+    z_own(1).start()
+    plane_start(2)
     z_wait(0)
     plane_start(0)
     plane_wait(2)
-    z_start(2)
-    z_wait(1)
-    plane_start(1)
+    z_start(2, Z_ORDER)
+    z_own(2).start()
+    plane_wait(0)
+    plane_start(3)
+    root_exchange(0)
+    root_section(0)
+    root_section(1)
     plane_wait(3)
-    z_start(3)
-    root_plane_last(0)
-    root_plane_last(1)
-    root_z_last(2)
-    root_z_last(3)
+    z_start(3, FAR)
+    z_own(3).start()
+    root_section(2)
+    z_start(3, NEAR)
+    root_section(3)
 
     for c in range(CHUNKS):
         for k in range(4):
@@ -268,7 +290,6 @@
         plane_all(c).wait_send()
         for k in range(NZ):
             pair2_copy(c, k, k).wait_send()
-        out_copy(c).wait()
 
 
 def per_device(vectors, leaf_factors, root_factors):
@@ -282,15 +303,15 @@
     out = pl.pallas_call(
         kernel,
         out_shape=jax.ShapeDtypeStruct(vectors.shape, bf),
-        in_specs=[pl.BlockSpec(memory_space=pl.ANY)] * 3,
-        out_specs=pl.BlockSpec(memory_space=pl.ANY),
+        in_specs=[pl.BlockSpec(memory_space=pltpu.HBM)] * 3,
+        out_specs=pl.BlockSpec(memory_space=pltpu.VMEM),
         scratch_shapes=[
             vmem((LEVELS, BLOCKS, BLK, 2 * BLK), bf),
             vmem((LEVELS, BLOCKS, BLK, 2 * BLK), bf),
             vmem(wide_shape, bf), vmem(halves, bf), vmem(halves, bf),
             vmem(spread, bf), vmem(spread, bf), vmem(spread, bf), vmem(spread, bf),
-            vmem(wide_shape[1:], bf), vmem(wide_shape[1:], bf), vmem(wide_shape, bf),
-            dma((CHUNKS,)), dma((LEVELS,)), dma((LEVELS,)), dma((CHUNKS,)), dma((CHUNKS, 2)),
+            vmem(wide_shape[1:], bf), vmem(wide_shape[1:], bf),
+            dma((CHUNKS,)), dma((LEVELS,)), dma((LEVELS,)), dma((CHUNKS, 2)),
             dma((CHUNKS, 4)), dma((CHUNKS, 4)), dma((CHUNKS, NZ - 1)), dma((CHUNKS, NZ - 1)),
             dma((CHUNKS,)), dma((CHUNKS,)), dma((CHUNKS, NZ)), dma((CHUNKS, NZ)),
         ],

time: 74.6 us -> 68.8 us (0.922)
  Pallas kernels: 71.6 us -> 65.7 us
    pallas_call x1, Pallas kernels: 71.6 us -> 65.7 us  [per_device(): pl.pallas_call(kernel, out_shape=jax.ShapeDtypeStruct(vectors.shape, bf),...]
where the time goes in v2:
time: 68.8 us; the launch traced here: 68.7 us
  Pallas kernels  65.7 us (95%)
  local copies, waits for them, and re-layouts  2.91 us (4%)
    pallas_call x1, Pallas kernels, per_device(): pl.pallas_call(kernel, out_shape=jax.ShapeDtypeStruct(vectors.shape, bf),...  65.7 us
    unnamed x3, local copies, waits for them, and re-layouts  2.91 us

profile of v2, /device:TPU:1, one launch (start us, length us, event | category | flops | bytes accessed | tf_op | source)
XLA Modules:
  0.0 68.7 jit_solution(11936859145884622470)
XLA Ops:
  0.0 0.0 copy-start
  0.0 1.6 %copy-done = bf16[2048,512]{1,0:T(8,128)(2,1)S(1)} copy-done((bf16[2048,512]{1,0:T(8,128)(2,1)S(1)}, bf16[2048,512]{1,0:T(8,128)(2,1)}, u32[]{:S(2)}) %copy-start) | copy-done | bytes 2097176
  1.6 65.7 %butterfly.1 = bf16[32,64,512]{2,1,0:T(8,128)(2,1)S(1)} custom-call(bf16[32,64,512]{2,1,0:T(8,128)(2,1)S(1)} %bitcast.3, bf16[6,32,64,128]{3,2,1,0:T(8,128)(2,1)} %leaf_hbm.1, bf16[6,32,64,128]{3,2,1,0:T(8,128)(2,1)} %root_hbm.1), custom_call_target="tpu_custom_call" | custom-call | tf_op jit(solution)/shard_map/butterfly/pallas_call | solution.py:303
  67.3 1.3 %copy.5 = bf16[2048,512]{1,0:T(8,128)(2,1)} copy(bf16[2048,512]{1,0:T(8,128)(2,1)S(1)} %bitcast.2) | data formatting | bytes 4194304
Async XLA Ops:
  0.0 1.6 %copy-start = (bf16[2048,512]{1,0:T(8,128)(2,1)S(1)}, bf16[2048,512]{1,0:T(8,128)(2,1)}, u32[]{:S(2)}) copy-start(bf16[2048,512]{1,0:T(8,128)(2,1)} %param.3) | copy-start | bytes 6291460

commit v3 on v2

--- a/solution.py
+++ b/solution.py
@@ -14,10 +14,22 @@
 PLANE_FIRST = (False, True, True, True)
 Z_ORDER = (4, 5, 3, 1, 7, 2, 6)
 FAR, NEAR = (4, 5, 3), (1, 7, 2, 6)
-BATCHES = ((0,) + FAR, NEAR)
+BATCHES = ((0,) + NEAR + FAR,)
 EARLY = 2
+UNROLL = 16
+LOOP = True
+
+
+def in_hbm(array):
+    return pltpu.with_memory_space_constraint(array, pltpu.HBM)
+
+
 RUN = ("L0", "L1", "L2", "L3", "P", "R0", "R1", "R2", "R3")
 own_copy = pltpu.make_async_copy
+
+
+def plane_first(c):
+    return PLANE_FIRST[c] if isinstance(c, int) else True
 
 
 def swap_halves(factor):
@@ -100,29 +112,29 @@
             pair_send.at[c, k], pair_recv.at[c, k], device_id=partner, device_id_type=MESH)
 
     def z_copy(c, d):
-        source, target = (half, moved) if PLANE_FIRST[c] else (leafed, half)
+        source, target = (half, moved) if plane_first(c) else (leafed, half)
         return pltpu.make_async_remote_copy(
             source.at[c, at_z(d)], target.at[c, z], z_send.at[c, d - 1], z_recv.at[c, d - 1],
             device_id=z_device(d), device_id_type=MESH)
 
     def z_own(c):
-        source, target = (half, moved) if PLANE_FIRST[c] else (leafed, half)
+        source, target = (half, moved) if plane_first(c) else (leafed, half)
         return own_copy(source.at[c, z], target.at[c, z], sem_own.at[c, 0])
 
     def plane_copy(c, j):
-        source, target = (leafed, half) if PLANE_FIRST[c] else (half, moved)
+        source, target = (leafed, half) if plane_first(c) else (half, moved)
         return pltpu.make_async_remote_copy(
             source.at[c, :, plane_at(j)], target.at[c, :, plane], plane_send.at[c], plane_recv.at[c],
             device_id=plane_device(j), device_id_type=MESH)
 
     def plane_all(c):
-        source, target = (leafed, half) if PLANE_FIRST[c] else (half, moved)
+        source, target = (leafed, half) if plane_first(c) else (half, moved)
         return pltpu.make_async_remote_copy(
             source.at[c, :, pl.ds(0, PLANE - 1)], target.at[c, :, pl.ds(0, PLANE - 1)],
             plane_send.at[c], plane_recv.at[c], device_id=partner, device_id_type=MESH)
 
     def plane_own(c):
-        source, target = (leafed, half) if PLANE_FIRST[c] else (half, moved)
+        source, target = (leafed, half) if plane_first(c) else (half, moved)
         return own_copy(source.at[c, :, plane], target.at[c, :, plane], sem_own.at[c, 1])
 
     def plane_start(c):
@@ -145,8 +157,15 @@
             device_id=partner, device_id_type=MESH)
 
     def whole_level(factors, source, target, stride):
-        for q in range(BLOCKS // 2):
-            pair_level(factors, source, target, first_of_pair(q, stride), stride)
+        if UNROLL == 16:
+            for q in range(BLOCKS // 2):
+                pair_level(factors, source, target, first_of_pair(q, stride), stride)
+            return
+
+        @pl.loop(0, BLOCKS // 2 // UNROLL)
+        def _(i):
+            for q in range(UNROLL):
+                pair_level(factors, source, target, first_of_pair(i * UNROLL + q, stride), stride)
 
     def leaf_levels(c):
         load_vec(c).wait()
@@ -205,7 +224,7 @@
     def root_rest(c):
         whole_level(root.at[3], ping2, pong2, 4)
         whole_level(root.at[4], pong2, ping2, 8)
-        whole_level(root.at[5], ping2, out.at[:, :, pl.ds(c * COLS, COLS)], 16)
+        whole_level(root.at[5], ping2, out.at[:, :, pl.ds(pl.multiple_of(c * COLS, COLS) if not isinstance(c, int) else c * COLS, COLS)], 16)
 
     def root_exchange(c):
         for k in range(NZ):
@@ -219,13 +238,13 @@
         root_rest(c)
 
     def root_z_last(c):
+        for d in sum(BATCHES, ()):
+            if d == 0:
+                z_own(c).wait()
+            else:
+                z_copy(c, d).wait_recv()
+            pair2_copy(c, (z - d) % NZ, d).start()
         for batch in BATCHES:
-            for d in batch:
-                if d == 0:
-                    z_own(c).wait()
-                else:
-                    z_copy(c, d).wait_recv()
-                pair2_copy(c, (z - d) % NZ, d).start()
             for d in batch:
                 pair2_copy(c, (z - d) % NZ, d).wait_recv()
             root_groups(c, [(z - d) % NZ for d in batch])
@@ -248,7 +267,7 @@
 
     def root_section(c):
         if f"R{c}" in RUN:
-            (root_z_last if PLANE_FIRST[c] else root_plane_last)(c)
+            (root_z_last if plane_first(c) else root_plane_last)(c)
 
     leaf_section(0)
     for l in range(LEVELS):
@@ -274,13 +293,22 @@
     plane_start(3)
     root_exchange(0)
     root_section(0)
-    root_section(1)
-    plane_wait(3)
-    z_start(3, FAR)
-    z_own(3).start()
-    root_section(2)
-    z_start(3, NEAR)
-    root_section(3)
+    if LOOP:
+        plane_wait(3)
+        z_start(3, Z_ORDER)
+        z_own(3).start()
+
+        @pl.loop(1, CHUNKS)
+        def _(c):
+            root_z_last(c)
+    else:
+        root_section(1)
+        plane_wait(3)
+        z_start(3, NEAR)
+        z_start(3, FAR)
+        z_own(3).start()
+        root_section(2)
+        root_section(3)
 
     for c in range(CHUNKS):
         for k in range(4):
@@ -318,7 +346,7 @@
         compiler_params=pltpu.CompilerParams(
             collective_id=0, has_side_effects=True, vmem_limit_bytes=48 * 1024 * 1024),
         name="butterfly",
-    )(vectors, leaf_factors, root_factors)
+    )(in_hbm(vectors), in_hbm(leaf_factors), in_hbm(root_factors))
     return out.reshape(BLOCKS * BLK, CHUNKS * COLS)
 
 

time: 68.8 us -> 67.1 us (0.975)
  local copies, waits for them, and re-layouts: 2.91 us -> 1.32 us
    unnamed x3 -> x1, local copies, waits for them, and re-layouts: 2.91 us -> 1.32 us
where the time goes in v3:
time: 67.1 us; the launch traced here: 67 us
  Pallas kernels  65.7 us (98%)
  local copies, waits for them, and re-layouts  1.32 us (2%)
    pallas_call x1, Pallas kernels, per_device(): pl.pallas_call(kernel, out_shape=jax.ShapeDtypeStruct(vectors.shape, bf),...  65.7 us

profile of v3, /device:TPU:1, one launch (start us, length us, event | category | flops | bytes accessed | tf_op | source)
XLA Modules:
  0.0 67.0 jit_solution(17870862098736605125)
XLA Ops:
  0.0 65.7 %butterfly.1 = bf16[32,64,512]{2,1,0:T(8,128)(2,1)S(1)} custom-call(bf16[32,64,512]{2,1,0:T(8,128)(2,1)} %bitcast.3, bf16[6,32,64,128]{3,2,1,0:T(8,128)(2,1)} %leaf_hbm.1, bf16[6,32,64,128]{3,2,1,0:T(8,128)(2,1)} %root_hbm.1), custom_call_target="tpu_custom_call" | custom-call | tf_op jit(solution)/shard_map/butterfly/pallas_call | solution.py:331
  65.7 1.3 %copy.5 = bf16[2048,512]{1,0:T(8,128)(2,1)} copy(bf16[2048,512]{1,0:T(8,128)(2,1)S(1)} %bitcast.2) | data formatting | bytes 4194304

commit v4 on v3

--- a/solution.py
+++ b/solution.py
@@ -15,9 +15,9 @@
 Z_ORDER = (4, 5, 3, 1, 7, 2, 6)
 FAR, NEAR = (4, 5, 3), (1, 7, 2, 6)
 BATCHES = ((0,) + NEAR + FAR,)
-EARLY = 2
+EARLY = 4
 UNROLL = 16
-LOOP = True
+LATE = 2
 
 
 def in_hbm(array):
@@ -238,16 +238,14 @@
         root_rest(c)
 
     def root_z_last(c):
-        for d in sum(BATCHES, ()):
-            if d == 0:
-                z_own(c).wait()
-            else:
-                z_copy(c, d).wait_recv()
+        z_own(c).wait()
+        pair2_copy(c, z, 0).start()
+        for d in NEAR + FAR:
+            z_copy(c, d).wait_recv()
             pair2_copy(c, (z - d) % NZ, d).start()
-        for batch in BATCHES:
-            for d in batch:
-                pair2_copy(c, (z - d) % NZ, d).wait_recv()
-            root_groups(c, [(z - d) % NZ for d in batch])
+        for d in (0,) + NEAR + FAR:
+            pair2_copy(c, (z - d) % NZ, d).wait_recv()
+        root_groups(c, range(NZ))
         root_rest(c)
 
     def z_wait(c):
@@ -293,22 +291,22 @@
     plane_start(3)
     root_exchange(0)
     root_section(0)
-    if LOOP:
-        plane_wait(3)
+    plane_wait(3)
+    z_own(3).start()
+    if not LATE:
         z_start(3, Z_ORDER)
-        z_own(3).start()
-
-        @pl.loop(1, CHUNKS)
-        def _(c):
-            root_z_last(c)
     else:
-        root_section(1)
-        plane_wait(3)
-        z_start(3, NEAR)
-        z_start(3, FAR)
-        z_own(3).start()
-        root_section(2)
-        root_section(3)
+        @pl.when(core == 0)
+        def _():
+            z_start(3, Z_ORDER)
+
+    @pl.loop(1, CHUNKS)
+    def _(c):
+        root_z_last(c)
+        if LATE:
+            @pl.when((core == 1) & (c == LATE))
+            def _():
+                z_start(3, Z_ORDER)
 
     for c in range(CHUNKS):
         for k in range(4):

time: 67.1 us -> 65.4 us (0.975)
  Pallas kernels: 65.7 us -> 63.9 us
    pallas_call x1, Pallas kernels: 65.7 us -> 63.9 us  [per_device(): pl.pallas_call(kernel, out_shape=jax.ShapeDtypeStruct(vectors.shape, bf),...]
where the time goes in v4:
time: 65.4 us; the launch traced here: 65.3 us
  Pallas kernels  63.9 us (98%)
  local copies, waits for them, and re-layouts  1.32 us (2%)
    pallas_call x1, Pallas kernels, per_device(): pl.pallas_call(kernel, out_shape=jax.ShapeDtypeStruct(vectors.shape, bf),...  63.9 us
    unnamed x1, local copies, waits for them, and re-layouts  1.32 us

profile of v4, /device:TPU:1, one launch (start us, length us, event | category | flops | bytes accessed | tf_op | source)
XLA Modules:
  0.0 65.3 jit_solution(5851264618387008496)
XLA Ops:
  0.0 63.9 %butterfly.1 = bf16[32,64,512]{2,1,0:T(8,128)(2,1)S(1)} custom-call(bf16[32,64,512]{2,1,0:T(8,128)(2,1)} %bitcast.3, bf16[6,32,64,128]{3,2,1,0:T(8,128)(2,1)} %leaf_hbm.1, bf16[6,32,64,128]{3,2,1,0:T(8,128)(2,1)} %root_hbm.1), custom_call_target="tpu_custom_call" | custom-call | tf_op jit(solution)/shard_map/butterfly/pallas_call | solution.py:329
  63.9 1.3 %copy.5 = bf16[2048,512]{1,0:T(8,128)(2,1)} copy(bf16[2048,512]{1,0:T(8,128)(2,1)S(1)} %bitcast.2) | data formatting | bytes 4194304

commit v5 on v4

--- a/solution.py
+++ b/solution.py
@@ -12,7 +12,7 @@
 GROUP = BLOCKS // NZ
 LEVELS = 6
 PLANE_FIRST = (False, True, True, True)
-Z_ORDER = (4, 5, 3, 1, 7, 2, 6)
+Z_ORDER = (4, 3, 5, 2, 6, 1, 7)
 FAR, NEAR = (4, 5, 3), (1, 7, 2, 6)
 BATCHES = ((0,) + NEAR + FAR,)
 EARLY = 4
@@ -185,25 +185,27 @@
             load_leaf(5).wait()
             for m in range(1, CHUNKS):
                 load_vec(m).start()
+        whole_level(leaf.at[4], ping.at[c], pong.at[c].reshape(BLOCKS, BLK, COLS), 16)
+        if c == 0:
             pl.semaphore_wait(barrier, 1 + (NZ - 1) + (PLANE - 1))
-        for k in range(4):
-            i = (z + k) % 4
-            for q in range(GROUP):
-                pair_level(leaf.at[4], ping.at[c], pong.at[c].reshape(BLOCKS, BLK, COLS), i * GROUP + q, 16)
-            pair_copy(c, i, k).start()
+        for i in range(4):
+            pair_copy(c, i, i).start()
 
     def leaf_last(c):
         mine = pong.at[c].reshape(BLOCKS, BLK, COLS)
         theirs = other.at[c].reshape(BLOCKS, BLK, COLS)
         target = leafed.at[c].reshape(BLOCKS, BLK, COLS)
-        for k, offsets in enumerate(((4,), (5, 1), (6, 2), (7, 3, 0))):
-            pair_copy(c, (z + k) % 4, k).wait_recv()
-            for d in offsets:
+        for i in range(4):
+            pair_copy(c, i, i).wait_recv()
+            for to in (i, i + 4):
                 for q in range(GROUP):
-                    b = at_z(d) * GROUP + q
+                    b = to * GROUP + q
                     target[b] = product(leaf[5, b], jnp.concatenate([mine[b], theirs[b]], axis=0))
-                if d != 0 and not PLANE_FIRST[c]:
-                    z_copy(c, d).start()
+            if not PLANE_FIRST[c]:
+                for to in (i, i + 4):
+                    @pl.when(z != to)
+                    def _():
+                        z_copy(c, (to - z) % NZ).start()
         if not PLANE_FIRST[c]:
             z_own(c).start()
 
@@ -310,7 +312,7 @@
 
     for c in range(CHUNKS):
         for k in range(4):
-            pair_copy(c, (z + k) % 4, k).wait_send()
+            pair_copy(c, k, k).wait_send()
         for d in Z_ORDER:
             z_copy(c, d).wait_send()
         plane_all(c).wait_send()

time: 65.4 us -> 65.4 us (level)
  no operation moved by 1% of the time
where the time goes in v5:
time: 65.4 us; the launch traced here: 65.3 us
  Pallas kernels  63.9 us (98%)
  local copies, waits for them, and re-layouts  1.32 us (2%)
    pallas_call x1, Pallas kernels, per_device(): pl.pallas_call(kernel, out_shape=jax.ShapeDtypeStruct(vectors.shape, bf),...  63.9 us
    unnamed x1, local copies, waits for them, and re-layouts  1.32 us

profile of v5, /device:TPU:1, one launch (start us, length us, event | category | flops | bytes accessed | tf_op | source)
XLA Modules:
  0.0 65.3 jit_solution(6073906947030443168)
XLA Ops:
  0.0 63.9 %butterfly.1 = bf16[32,64,512]{2,1,0:T(8,128)(2,1)S(1)} custom-call(bf16[32,64,512]{2,1,0:T(8,128)(2,1)} %bitcast.3, bf16[6,32,64,128]{3,2,1,0:T(8,128)(2,1)} %leaf_hbm.1, bf16[6,32,64,128]{3,2,1,0:T(8,128)(2,1)} %root_hbm.1), custom_call_target="tpu_custom_call" | custom-call | tf_op jit(solution)/shard_map/butterfly/pallas_call | solution.py:331
  63.9 1.3 %copy.5 = bf16[2048,512]{1,0:T(8,128)(2,1)} copy(bf16[2048,512]{1,0:T(8,128)(2,1)S(1)} %bitcast.2) | data formatting | bytes 4194304

commit v6 on v5

--- a/solution.py
+++ b/solution.py
@@ -302,6 +302,18 @@
         def _():
             z_start(3, Z_ORDER)
 
+    def sent(c):
+        for d in Z_ORDER:
+            z_copy(c, d).wait_send()
+        for k in range(NZ):
+            pair2_copy(c, k, k).wait_send()
+
+    for c in range(CHUNKS):
+        for k in range(4):
+            pair_copy(c, k, k).wait_send()
+        plane_all(c).wait_send()
+    sent(0)
+
     @pl.loop(1, CHUNKS)
     def _(c):
         root_z_last(c)
@@ -310,14 +322,7 @@
             def _():
                 z_start(3, Z_ORDER)
 
-    for c in range(CHUNKS):
-        for k in range(4):
-            pair_copy(c, k, k).wait_send()
-        for d in Z_ORDER:
-            z_copy(c, d).wait_send()
-        plane_all(c).wait_send()
-        for k in range(NZ):
-            pair2_copy(c, k, k).wait_send()
+        sent(c)
 
 
 def per_device(vectors, leaf_factors, root_factors):

time: 65.4 us -> 65.3 us (level)
  no operation moved by 1% of the time
where the time goes in v6:
time: 65.3 us; the launch traced here: 65.2 us
  Pallas kernels  63.8 us (98%)
  local copies, waits for them, and re-layouts  1.32 us (2%)
    pallas_call x1, Pallas kernels, per_device(): pl.pallas_call(kernel, out_shape=jax.ShapeDtypeStruct(vectors.shape, bf),...  63.8 us
    unnamed x1, local copies, waits for them, and re-layouts  1.32 us

profile of v6, /device:TPU:1, one launch (start us, length us, event | category | flops | bytes accessed | tf_op | source)
XLA Modules:
  0.0 65.2 jit_solution(13780111046124534423)
XLA Ops:
  0.0 63.8 %butterfly.1 = bf16[32,64,512]{2,1,0:T(8,128)(2,1)S(1)} custom-call(bf16[32,64,512]{2,1,0:T(8,128)(2,1)} %bitcast.3, bf16[6,32,64,128]{3,2,1,0:T(8,128)(2,1)} %leaf_hbm.1, bf16[6,32,64,128]{3,2,1,0:T(8,128)(2,1)} %root_hbm.1), custom_call_target="tpu_custom_call" | custom-call | tf_op jit(solution)/shard_map/butterfly/pallas_call | solution.py:336
  63.8 1.3 %copy.5 = bf16[2048,512]{1,0:T(8,128)(2,1)} copy(bf16[2048,512]{1,0:T(8,128)(2,1)S(1)} %bitcast.2) | data formatting | bytes 4194304

commit v7 on v6

--- a/solution.py
+++ b/solution.py
@@ -188,24 +188,23 @@
         whole_level(leaf.at[4], ping.at[c], pong.at[c].reshape(BLOCKS, BLK, COLS), 16)
         if c == 0:
             pl.semaphore_wait(barrier, 1 + (NZ - 1) + (PLANE - 1))
-        for i in range(4):
+        for k in (0, 1, 3, 2):
+            i = (z + k) % 4
             pair_copy(c, i, i).start()
 
     def leaf_last(c):
         mine = pong.at[c].reshape(BLOCKS, BLK, COLS)
         theirs = other.at[c].reshape(BLOCKS, BLK, COLS)
         target = leafed.at[c].reshape(BLOCKS, BLK, COLS)
-        for i in range(4):
+        for k in (0, 1, 3, 2):
+            i = (z + k) % 4
             pair_copy(c, i, i).wait_recv()
-            for to in (i, i + 4):
+            for d in (k, k + 4):
                 for q in range(GROUP):
-                    b = to * GROUP + q
+                    b = at_z(d) * GROUP + q
                     target[b] = product(leaf[5, b], jnp.concatenate([mine[b], theirs[b]], axis=0))
             if not PLANE_FIRST[c]:
-                for to in (i, i + 4):
-                    @pl.when(z != to)
-                    def _():
-                        z_copy(c, (to - z) % NZ).start()
+                z_start(c, {0: (4,), 1: (5,), 3: (3,), 2: (2, 6, 1, 7)}[k])
         if not PLANE_FIRST[c]:
             z_own(c).start()
 

time: 65.3 us -> 65.3 us (level)
  no operation moved by 1% of the time
where the time goes in v7:
time: 65.3 us; the launch traced here: 65.2 us
  Pallas kernels  63.9 us (98%)
  local copies, waits for them, and re-layouts  1.32 us (2%)
    pallas_call x1, Pallas kernels, per_device(): pl.pallas_call(kernel, out_shape=jax.ShapeDtypeStruct(vectors.shape, bf),...  63.9 us
    unnamed x1, local copies, waits for them, and re-layouts  1.32 us

profile of v7, /device:TPU:1, one launch (start us, length us, event | category | flops | bytes accessed | tf_op | source)
XLA Modules:
  0.0 65.2 jit_solution(18376069687338191445)
XLA Ops:
  0.0 63.9 %butterfly.1 = bf16[32,64,512]{2,1,0:T(8,128)(2,1)S(1)} custom-call(bf16[32,64,512]{2,1,0:T(8,128)(2,1)} %bitcast.3, bf16[6,32,64,128]{3,2,1,0:T(8,128)(2,1)} %leaf_hbm.1, bf16[6,32,64,128]{3,2,1,0:T(8,128)(2,1)} %root_hbm.1), custom_call_target="tpu_custom_call" | custom-call | tf_op jit(solution)/shard_map/butterfly/pallas_call | solution.py:335
  63.9 1.3 %copy.5 = bf16[2048,512]{1,0:T(8,128)(2,1)} copy(bf16[2048,512]{1,0:T(8,128)(2,1)S(1)} %bitcast.2) | data formatting | bytes 4194304
